TPU v7x, 32 devices: a whole 2x2x4 slice. The times are simulated.
32 devices in a mesh: grp: 2 (over x), row: 16 (over z, y, core).
Axes of the slice: x: 2, y: 2, z: 4, core: 2. Of those that a mesh axis runs over, the one named last changes fastest.
Arguments:
- features: bfloat16 [16384, 768], P(('grp', 'row')), parts along dimension 0, may hold values from -6 to 6
- degree: int32 [16384], P(('grp', 'row')), parts along dimension 0, may hold values from 8 to 63
- block_list: int32 [576, 2], P(('grp', 'row')), parts along dimension 0, may hold values from 0 to 31, as said below
- block_count: int32 [32], P(('grp', 'row')), parts along dimension 0, may hold values from 12 to 18, as said below
- tiles: bfloat16 [576, 256, 256], P(('grp', 'row')), parts along dimension 0, may hold values from 0 to 1
- self_weight: bfloat16 [768, 512], replicated, may hold values from -0.21875 to 0.21875
- neigh_weight: bfloat16 [768, 512], replicated, may hold values from -0.21875 to 0.21875
- bias: float32 [512], replicated, may hold values from -3 to 3
- cotangent: bfloat16 [16384, 512], P(('grp', 'row')), parts along dimension 0, may hold values from -6 to 6
Outputs:
- activated: bfloat16 [16384, 512], P(('grp', 'row')), parts along dimension 0
- grad_features: bfloat16 [16384, 768], P(('grp', 'row')), parts along dimension 0
- grad_self: float32 [1536, 512], P('grp'), parts along dimension 0
- grad_neigh: float32 [1536, 512], P('grp'), parts along dimension 0
- grad_bias: float32 [1024], P('grp'), parts along dimension 0
There are 2 independent parts, one for each index of `grp`. A program takes and returns all parts, laid end to end along the dimension named above; an argument that names none is the same for every part. Nothing has to cross between parts.
Inputs may be any that keep to these rules, and one draw needn't show every extreme that they name: `block_list`: column 0 of a slot is a row tile among the 2 tile rows of the device that holds the slot; column 1 is a column tile among the tile rows of the devices up to 4 away along row, counted cyclically over 32 tile rows. The 18 slots of a device name distinct column tiles, so all of them together cover that device's whole reach. `block_count`: the live slots of a device are its leading ones; some device has all 18 live.
All inputs are finite; a program needn't handle non-finite values.
Results may differ from a plain program's by a relative error of at most 0.0059.
Values may be sent and summed in bfloat16 or wider, within the bound.
A program may use at most 64 MiB of HBM per device.

v0:
```python
import jax
import jax.numpy as jnp
from jax import lax
from jax.sharding import PartitionSpec as P

HOPS = 4


def from_behind(block, axis, distance):
    devices = range(lax.axis_size(axis))
    route = [((i - distance) % len(devices), i) for i in devices]
    return lax.ppermute(block, axis, route)


def smooth_gate(values):
    return jax.nn.gelu(values, approximate=True)


def on_device(
    features, degree, block_list, block_count, tiles, self_weight, neigh_weight, bias, cotangent
):
    rows_dev = features.shape[0]
    tile_size = tiles.shape[1]
    trows = rows_dev // tile_size
    width = neigh_weight.shape[1]
    device = lax.axis_index("row")
    total_tiles = trows * lax.axis_size("row")
    window_start = (device - HOPS) * trows
    row_slot = block_list[:, 0] - device * trows
    window_slot = (block_list[:, 1] - window_start) % total_tiles
    live_count = block_count[0]
    projected = jnp.dot(features, neigh_weight, preferred_element_type=jnp.float32).astype(
        jnp.bfloat16
    )
    proj_tiles = projected.reshape(trows, tile_size, width)
    pieces = {0: proj_tiles}
    for offset in range(-HOPS, HOPS + 1):
        if offset != 0:
            pieces[offset] = from_behind(proj_tiles, "row", -offset)
    window = jnp.concatenate([pieces[offset] for offset in range(-HOPS, HOPS + 1)], axis=0)

    def forward_block(block, gathered):
        source = lax.dynamic_index_in_dim(window, window_slot[block], 0, keepdims=False)
        partial_value = jnp.dot(tiles[block], source, preferred_element_type=jnp.float32)
        return gathered.at[row_slot[block]].add(partial_value)

    summed = lax.fori_loop(
        0, live_count, forward_block, jnp.zeros((trows, tile_size, width), jnp.float32)
    )
    scale = degree.astype(jnp.float32)[:, None]
    pre = (
        jnp.dot(features, self_weight, preferred_element_type=jnp.float32)
        + summed.reshape(rows_dev, width) / scale
        + bias[None, :]
    )
    activated, pullback = jax.vjp(smooth_gate, pre)
    grad_pre = pullback(cotangent.astype(jnp.float32))[0]
    message = (grad_pre / scale).astype(jnp.bfloat16).reshape(trows, tile_size, width)

    def backward_block(block, gathered):
        source = lax.dynamic_index_in_dim(message, row_slot[block], 0, keepdims=False)
        partial_value = lax.dot_general(
            tiles[block], source, (((0,), (0,)), ((), ())), preferred_element_type=jnp.float32
        )
        return gathered.at[window_slot[block]].add(partial_value)

    span = 2 * HOPS + 1
    back_terms = lax.fori_loop(
        0, live_count, backward_block, jnp.zeros((span * trows, tile_size, width), jnp.float32)
    )
    back_terms = back_terms.reshape(span, trows, tile_size, width)
    received = back_terms[HOPS]
    for offset in range(-HOPS, HOPS + 1):
        if offset != 0:
            received = received + from_behind(back_terms[HOPS + offset], "row", offset)
    grad_proj = received.reshape(rows_dev, width)
    grad_pre_b = grad_pre.astype(jnp.bfloat16)
    grad_proj_b = grad_proj.astype(jnp.bfloat16)
    contract_out = (((1,), (1,)), ((), ()))
    grad_features = (
        lax.dot_general(grad_pre_b, self_weight, contract_out, preferred_element_type=jnp.float32)
        + lax.dot_general(
            grad_proj_b, neigh_weight, contract_out, preferred_element_type=jnp.float32
        )
    ).astype(jnp.bfloat16)
    contract_rows = (((0,), (0,)), ((), ()))
    local_self = lax.dot_general(
        features, grad_pre_b, contract_rows, preferred_element_type=jnp.float32
    )
    local_neigh = lax.dot_general(
        features, grad_proj_b, contract_rows, preferred_element_type=jnp.float32
    )
    local_bias = jnp.sum(grad_pre, axis=0)
    grad_self, grad_neigh, grad_bias = lax.psum((local_self, local_neigh, local_bias), "row")
    return (activated.astype(jnp.bfloat16), grad_features, grad_self, grad_neigh, grad_bias)


def solution(mesh):
    return jax.shard_map(
        on_device,
        mesh=mesh,
        in_specs=(
            P(("grp", "row"), None),
            P(("grp", "row")),
            P(("grp", "row"), None),
            P(("grp", "row")),
            P(("grp", "row"), None, None),
            P(),
            P(),
            P(),
            P(("grp", "row"), None),
        ),
        out_specs=(
            P(("grp", "row"), None),
            P(("grp", "row"), None),
            P("grp", None),
            P("grp", None),
            P("grp"),
        ),
        check_vma=False,
    )
```

profile of v0, /device:TPU:1, one launch (start us, length us, event | category | flops | bytes accessed | tf_op | source)
XLA Modules:
  0.0 656.2 jit_solution(6049465066602393732)
XLA Ops:
  10.0 2.2 collective-permute-start
  12.2 2.1 collective-permute-start.1
  18.5 7.5 %collective-permute-done = bf16[2,256,512]{2,1,0:T(8,128)(2,1)} collective-permute-done((bf16[2,256,512]{2,1,0:T(8,128)(2,1)S(1)}, bf16[2,256,512]{2,1,0:T(8,128)(2,1)}, u32[]{:S(2)}, u32[]{:S(2)}) %collective-permute-start) | collective-permute-done | bytes 524320 | tf_op jit(solution)/shard_map/ppermute | solution.py:12
  26.0 2.1 collective-permute-start.5
  29.2 10.6 %collective-permute-done.1 = bf16[2,256,512]{2,1,0:T(8,128)(2,1)S(1)} collective-permute-done((bf16[2,256,512]{2,1,0:T(8,128)(2,1)S(1)}, bf16[2,256,512]{2,1,0:T(8,128)(2,1)S(1)}, u32[]{:S(2)}, u32[]{:S(2)}) %collective-permute-start.1) | collective-permute-done | bytes 524320 | tf_op jit(solution)/shard_map/ppermute | solution.py:12
  39.8 9.3 %collective-permute-done.2 = bf16[2,256,512]{2,1,0:T(8,128)(2,1)S(1)} collective-permute-done((bf16[2,256,512]{2,1,0:T(8,128)(2,1)S(1)}, bf16[2,256,512]{2,1,0:T(8,128)(2,1)S(1)}, u32[]{:S(2)}, u32[]{:S(2)}) %collective-permute-start.2) | collective-permute-done | bytes 524320 | tf_op jit(solution)/shard_map/ppermute | solution.py:12
  50.5 8.9 %collective-permute-done.3 = bf16[2,256,512]{2,1,0:T(8,128)(2,1)S(1)} collective-permute-done((bf16[2,256,512]{2,1,0:T(8,128)(2,1)S(1)}, bf16[2,256,512]{2,1,0:T(8,128)(2,1)S(1)}, u32[]{:S(2)}, u32[]{:S(2)}) %collective-permute-start.3) | collective-permute-done | bytes 524320 | tf_op jit(solution)/shard_map/ppermute | solution.py:12
  61.1 4.0 collective-permute-done.6
  65.1 2.0 collective-permute-done.7
  67.2 2.0 copy-done.3
  69.2 117.6 %while.22 = (s32[]{:T(128)}, f32[2,256,512]{2,1,0:T(8,128)S(1)}, s32[]{:T(128)}, s32[18]{0:T(128)S(1)}, bf16[18,256,256]{2,1,0:T(8,128)(2,1)}, /*index=5*/s32[18...) while((s32[]{:T(128)}, f32[2,256,512]{2,1,0:T(8,128)S(1)}, ...), condition=%wide.region_2.3_spmd, body=%wide.region_0.2_spmd.sunk | while | flops 67371032 | bytes 1443096 | solution.py:47
  84.1 1.9 fusion.51
  100.8 1.9 fusion.51
  117.5 1.9 fusion.51
  134.2 1.9 fusion.51
  150.9 1.9 fusion.51
  167.6 1.9 fusion.51
  187.0 2.1 fusion.30
  189.3 4.9 broadcast_in_dim.6
  194.2 130.4 %while.23 = (s32[]{:T(128)}, f32[18,256,512]{2,1,0:T(8,128)}, s32[]{:T(128)}, s32[18]{0:T(128)S(1)}, bf16[18,256,256]{2,1,0:T(8,128)(2,1)}, /*index=5*/s32[18]{0...) while((s32[]{:T(128)}, f32[18,256,512]{2,1,0:T(8,128)}, ...), condition=%wide.region_5.6_spmd, body=%wide.region_3.5_spmd.sunk | while | flops 67371032 | bytes 1443096 | solution.py:68
  200.6 2.8 fusion.54
  209.9 2.9 fusion.54
  219.2 2.8 fusion.54
  228.5 2.8 fusion.54
  237.7 2.8 fusion.54
  247.0 2.8 fusion.54
  256.2 2.9 fusion.54
  265.5 2.8 fusion.54
  274.8 2.8 fusion.54
  284.1 2.8 fusion.54
  293.3 2.8 fusion.54
  302.6 2.8 fusion.54
  311.9 2.8 fusion.54
  321.1 2.8 fusion.54
  324.6 4.4 fusion.32
  329.1 29.4 %collective-permute-start.10 = (f32[2,256,512]{2,1,0:T(8,128)S(1)}, f32[2,256,512]{2,1,0:T(8,128)S(1)}, u32[]{:S(2)}, u32[]{:S(2)}) collective-permute-start(f32[2,256,512]{2,1,0:T(8,128)S(1)} %get-tuple-element.150), channel_id=1, source_target_pairs={{2,0},{3,1},{4,2},{5,3},{6,4},{7,5},{8,6},{9,7},{10,8},{11,9},{12,... | collective-permute-start | bytes 3145736 | tf_op jit(solution)/shard_map/ppermute | solution.py:12
  358.5 30.5 %collective-permute-start.11 = (f32[2,256,512]{2,1,0:T(8,128)S(1)}, f32[2,256,512]{2,1,0:T(8,128)S(1)}, u32[]{:S(2)}, u32[]{:S(2)}) collective-permute-start(f32[2,256,512]{2,1,0:T(8,128)S(1)} %get-tuple-element.149), channel_id=1, source_target_pairs={{1,0},{2,1},{3,2},{4,3},{5,4},{6,5},{7,6},{8,7},{9,8},{10,9},{11,1... | collective-permute-start | bytes 3145736 | tf_op jit(solution)/shard_map/ppermute | solution.py:12
  389.1 24.8 %collective-permute-start.13 = (f32[2,256,512]{2,1,0:T(8,128)S(1)}, f32[2,256,512]{2,1,0:T(8,128)S(1)}, u32[]{:S(2)}, u32[]{:S(2)}) collective-permute-start(f32[2,256,512]{2,1,0:T(8,128)S(1)} %get-tuple-element.147), channel_id=1, source_target_pairs={{14,0},{15,1},{0,2},{1,3},{2,4},{3,5},{4,6},{5,7},{6,8},{7,9},{8,1... | collective-permute-start | bytes 3145736 | tf_op jit(solution)/shard_map/ppermute | solution.py:12
  415.1 54.6 %collective-permute-start.15 = (f32[2,256,512]{2,1,0:T(8,128)S(1)}, f32[2,256,512]{2,1,0:T(8,128)S(1)}, u32[]{:S(2)}, u32[]{:S(2)}) collective-permute-start(f32[2,256,512]{2,1,0:T(8,128)S(1)} %get-tuple-element.145), channel_id=1, source_target_pairs={{12,0},{13,1},{14,2},{15,3},{0,4},{1,5},{2,6},{3,7},{4,8},{5,9},{6... | collective-permute-start | bytes 3145736 | tf_op jit(solution)/shard_map/ppermute | solution.py:12
  469.7 13.9 %collective-permute-start.8 = (f32[2,256,512]{2,1,0:T(8,128)S(1)}, f32[2,256,512]{2,1,0:T(8,128)S(1)}, u32[]{:S(2)}, u32[]{:S(2)}) collective-permute-start(f32[2,256,512]{2,1,0:T(8,128)S(1)} %get-tuple-element.144), channel_id=1, source_target_pairs={{4,0},{5,1},{6,2},{7,3},{8,4},{9,5},{10,6},{11,7},{12,8},{13,9},{1... | collective-permute-start | bytes 3145736 | tf_op jit(solution)/shard_map/ppermute | solution.py:12
  485.4 3.9 collective-permute-done.15
  489.3 28.1 %collective-permute-done.8 = f32[2,256,512]{2,1,0:T(8,128)S(1)} collective-permute-done((f32[2,256,512]{2,1,0:T(8,128)S(1)}, f32[2,256,512]{2,1,0:T(8,128)S(1)}, u32[]{:S(2)}, u32[]{:S(2)}) %collective-permute-start.8) | collective-permute-done | bytes 1048608 | tf_op jit(solution)/shard_map/ppermute | solution.py:12
  517.4 12.5 %collective-permute-done.9 = f32[2,256,512]{2,1,0:T(8,128)S(1)} collective-permute-done((f32[2,256,512]{2,1,0:T(8,128)S(1)}, f32[2,256,512]{2,1,0:T(8,128)S(1)}, u32[]{:S(2)}, u32[]{:S(2)}) %collective-permute-start.9) | collective-permute-done | bytes 1048608 | tf_op jit(solution)/shard_map/ppermute | solution.py:12
  529.9 2.2 add_convert_fusion.1
  533.9 38.2 %psum.23 = f32[512]{0:T(512)} all-reduce(f32[512]{0:T(512)S(1)} %get-tuple-element.142), channel_id=1, replica_groups=mesh['grp'=2,'row'=16] {'row'}, use_global_device_ids=true, to_apply=%region_9.10 | all-reduce | flops 512 | bytes 4096 | tf_op jit(solution)/shard_map/psum | solution.py:94
  575.4 68.0 %all-reduce.3.cloned.1.call-done = (f32[768,512]{0,1:T(8,128)}, f32[768,512]{0,1:T(8,128)}) async-done(((f32[768,512]{0,1:T(8,128)}, f32[768,512]{0,1:T(8,128)}), (f32[768,512]{0,1:T(8,128)}, f32[768,512]{0,1:T(8,128)})) %all-reduce.3.cloned.1.call-update) | async-done | bytes 3145744 | tf_op jit(solution)/shard_map/psum | solution.py:94
  643.4 3.0 copy.14
  646.4 3.0 copy.15
  (144 shorter events, 87.6 us)
Async XLA Ops:
  7.2 1.1 copy-start
  7.2 636.2 %all-reduce.3.cloned.1.call-start = ((), (), s32[]{:S(2)}) async-start(), calls=%async_computation | async-start | bytes 6291456 | tf_op jit(solution)/shard_map/psum | solution.py:94
  10.0 16.0 %collective-permute-start = (bf16[2,256,512]{2,1,0:T(8,128)(2,1)S(1)}, bf16[2,256,512]{2,1,0:T(8,128)(2,1)}, u32[]{:S(2)}, u32[]{:S(2)}) collective-permute-start(bf16[2,256,512]{2,1,0:T(8,128)(2,1)S(1)} %bitcast.85), channel_id=1, source_target_pairs={{12,0},{13,1},{14,2},{15,3},{0,4},{1,5},{2,6},{3,7},{4,8},{5,9},{6... | collective-permute-start | bytes 1572872 | tf_op jit(solution)/shard_map/ppermute | solution.py:12
  12.2 27.6 %collective-permute-start.1 = (bf16[2,256,512]{2,1,0:T(8,128)(2,1)S(1)}, bf16[2,256,512]{2,1,0:T(8,128)(2,1)S(1)}, u32[]{:S(2)}, u32[]{:S(2)}) collective-permute-start(bf16[2,256,512]{2,1,0:T(8,128)(2,1)S(1)} %bitcast.86), channel_id=1, source_target_pairs={{13,0},{14,1},{15,2},{0,3},{1,4},{2,5},{3,6},{4,7},{5,8},{6,9},{7,... | collective-permute-start | bytes 1572872 | tf_op jit(solution)/shard_map/ppermute | solution.py:12
  14.3 34.8 %collective-permute-start.2 = (bf16[2,256,512]{2,1,0:T(8,128)(2,1)S(1)}, bf16[2,256,512]{2,1,0:T(8,128)(2,1)S(1)}, u32[]{:S(2)}, u32[]{:S(2)}) collective-permute-start(bf16[2,256,512]{2,1,0:T(8,128)(2,1)S(1)} %bitcast.87), channel_id=1, source_target_pairs={{14,0},{15,1},{0,2},{1,3},{2,4},{3,5},{4,6},{5,7},{6,8},{7,9},{8,1... | collective-permute-start | bytes 1572872 | tf_op jit(solution)/shard_map/ppermute | solution.py:12
  15.6 43.9 %collective-permute-start.3 = (bf16[2,256,512]{2,1,0:T(8,128)(2,1)S(1)}, bf16[2,256,512]{2,1,0:T(8,128)(2,1)S(1)}, u32[]{:S(2)}, u32[]{:S(2)}) collective-permute-start(bf16[2,256,512]{2,1,0:T(8,128)(2,1)S(1)} %bitcast.88), channel_id=1, source_target_pairs={{15,0},{0,1},{1,2},{2,3},{3,4},{4,5},{5,6},{6,7},{7,8},{8,9},{9,10... | collective-permute-start | bytes 1572872 | tf_op jit(solution)/shard_map/ppermute | solution.py:12
  16.5 43.1 %collective-permute-start.4 = (bf16[2,256,512]{2,1,0:T(8,128)(2,1)S(1)}, bf16[2,256,512]{2,1,0:T(8,128)(2,1)S(1)}, u32[]{:S(2)}, u32[]{:S(2)}) collective-permute-start(bf16[2,256,512]{2,1,0:T(8,128)(2,1)S(1)} %bitcast.89), channel_id=1, source_target_pairs={{1,0},{2,1},{3,2},{4,3},{5,4},{6,5},{7,6},{8,7},{9,8},{10,9},{11,1... | collective-permute-start | bytes 1572872 | tf_op jit(solution)/shard_map/ppermute | solution.py:12
  26.0 35.0 %collective-permute-start.5 = (bf16[2,256,512]{2,1,0:T(8,128)(2,1)S(1)}, bf16[2,256,512]{2,1,0:T(8,128)(2,1)S(1)}, u32[]{:S(2)}, u32[]{:S(2)}) collective-permute-start(bf16[2,256,512]{2,1,0:T(8,128)(2,1)S(1)} %bitcast.90), channel_id=1, source_target_pairs={{2,0},{3,1},{4,2},{5,3},{6,4},{7,5},{8,6},{9,7},{10,8},{11,9},{12,... | collective-permute-start | bytes 1572872 | tf_op jit(solution)/shard_map/ppermute | solution.py:12
  29.1 40.1 %copy-start.5 = (s32[3]{0:T(128)S(1)}, s32[3]{0:T(128)}, u32[]{:S(2)}) copy-start(s32[3]{0:T(128)} %constant.88.clone.1) | copy-start | bytes 40
  39.8 25.3 %collective-permute-start.6 = (bf16[2,256,512]{2,1,0:T(8,128)(2,1)S(1)}, bf16[2,256,512]{2,1,0:T(8,128)(2,1)S(1)}, u32[]{:S(2)}, u32[]{:S(2)}) collective-permute-start(bf16[2,256,512]{2,1,0:T(8,128)(2,1)S(1)} %bitcast.91), channel_id=1, source_target_pairs={{3,0},{4,1},{5,2},{6,3},{7,4},{8,5},{9,6},{10,7},{11,8},{12,9},{13... | collective-permute-start | bytes 1572872 | tf_op jit(solution)/shard_map/ppermute | solution.py:12
  49.1 18.0 %collective-permute-start.7 = (bf16[2,256,512]{2,1,0:T(8,128)(2,1)S(1)}, bf16[2,256,512]{2,1,0:T(8,128)(2,1)S(1)}, u32[]{:S(2)}, u32[]{:S(2)}) collective-permute-start(bf16[2,256,512]{2,1,0:T(8,128)(2,1)S(1)} %bitcast.92), channel_id=1, source_target_pairs={{4,0},{5,1},{6,2},{7,3},{8,4},{9,5},{10,6},{11,7},{12,8},{13,9},{1... | collective-permute-start | bytes 1572872 | tf_op jit(solution)/shard_map/ppermute | solution.py:12
  67.1 2.1 copy-start.3
  69.2 117.8 %copy-start.2 = (bf16[768,512]{1,0:T(8,128)(2,1)S(1)}, bf16[768,512]{1,0:T(8,128)(2,1)}, u32[]{:S(2)}) copy-start(bf16[768,512]{1,0:T(8,128)(2,1)} %param.22) | copy-start | bytes 2359300
  69.2 117.8 %copy-start.6 = (bf16[512,512]{1,0:T(8,128)(2,1)S(1)}, bf16[512,512]{1,0:T(8,128)(2,1)}, u32[]{:S(2)}) copy-start(bf16[512,512]{1,0:T(8,128)(2,1)} %param.25) | copy-start | bytes 1572868
  69.2 117.8 %copy-start.7 = (f32[512]{0:T(512)S(1)}, f32[512]{0:T(512)}, u32[]{:S(2)}) copy-start(f32[512]{0:T(512)} %param.24) | copy-start | bytes 6148
  189.3 4.9 copy-start.4
  329.1 86.0 %collective-permute-start.10 = (f32[2,256,512]{2,1,0:T(8,128)S(1)}, f32[2,256,512]{2,1,0:T(8,128)S(1)}, u32[]{:S(2)}, u32[]{:S(2)}) collective-permute-start(f32[2,256,512]{2,1,0:T(8,128)S(1)} %get-tuple-element.150), channel_id=1, source_target_pairs={{2,0},{3,1},{4,2},{5,3},{6,4},{7,5},{8,6},{9,7},{10,8},{11,9},{12,... | collective-permute-start | bytes 3145736 | tf_op jit(solution)/shard_map/ppermute | solution.py:12
  358.5 111.2 %collective-permute-start.11 = (f32[2,256,512]{2,1,0:T(8,128)S(1)}, f32[2,256,512]{2,1,0:T(8,128)S(1)}, u32[]{:S(2)}, u32[]{:S(2)}) collective-permute-start(f32[2,256,512]{2,1,0:T(8,128)S(1)} %get-tuple-element.149), channel_id=1, source_target_pairs={{1,0},{2,1},{3,2},{4,3},{5,4},{6,5},{7,6},{8,7},{9,8},{10,9},{11,1... | collective-permute-start | bytes 3145736 | tf_op jit(solution)/shard_map/ppermute | solution.py:12
  389.0 94.6 %collective-permute-start.12 = (f32[2,256,512]{2,1,0:T(8,128)S(1)}, f32[2,256,512]{2,1,0:T(8,128)S(1)}, u32[]{:S(2)}, u32[]{:S(2)}) collective-permute-start(f32[2,256,512]{2,1,0:T(8,128)S(1)} %get-tuple-element.148), channel_id=1, source_target_pairs={{15,0},{0,1},{1,2},{2,3},{3,4},{4,5},{5,6},{6,7},{7,8},{8,9},{9,10... | collective-permute-start | bytes 3145736 | tf_op jit(solution)/shard_map/ppermute | solution.py:12
  389.1 96.3 %collective-permute-start.13 = (f32[2,256,512]{2,1,0:T(8,128)S(1)}, f32[2,256,512]{2,1,0:T(8,128)S(1)}, u32[]{:S(2)}, u32[]{:S(2)}) collective-permute-start(f32[2,256,512]{2,1,0:T(8,128)S(1)} %get-tuple-element.147), channel_id=1, source_target_pairs={{14,0},{15,1},{0,2},{1,3},{2,4},{3,5},{4,6},{5,7},{6,8},{7,9},{8,1... | collective-permute-start | bytes 3145736 | tf_op jit(solution)/shard_map/ppermute | solution.py:12
  413.9 71.5 %collective-permute-start.14 = (f32[2,256,512]{2,1,0:T(8,128)S(1)}, f32[2,256,512]{2,1,0:T(8,128)S(1)}, u32[]{:S(2)}, u32[]{:S(2)}) collective-permute-start(f32[2,256,512]{2,1,0:T(8,128)S(1)} %get-tuple-element.146), channel_id=1, source_target_pairs={{13,0},{14,1},{15,2},{0,3},{1,4},{2,5},{3,6},{4,7},{5,8},{6,9},{7,... | collective-permute-start | bytes 3145736 | tf_op jit(solution)/shard_map/ppermute | solution.py:12
  415.1 74.2 %collective-permute-start.15 = (f32[2,256,512]{2,1,0:T(8,128)S(1)}, f32[2,256,512]{2,1,0:T(8,128)S(1)}, u32[]{:S(2)}, u32[]{:S(2)}) collective-permute-start(f32[2,256,512]{2,1,0:T(8,128)S(1)} %get-tuple-element.145), channel_id=1, source_target_pairs={{12,0},{13,1},{14,2},{15,3},{0,4},{1,5},{2,6},{3,7},{4,8},{5,9},{6... | collective-permute-start | bytes 3145736 | tf_op jit(solution)/shard_map/ppermute | solution.py:12
  469.7 47.7 %collective-permute-start.8 = (f32[2,256,512]{2,1,0:T(8,128)S(1)}, f32[2,256,512]{2,1,0:T(8,128)S(1)}, u32[]{:S(2)}, u32[]{:S(2)}) collective-permute-start(f32[2,256,512]{2,1,0:T(8,128)S(1)} %get-tuple-element.144), channel_id=1, source_target_pairs={{4,0},{5,1},{6,2},{7,3},{8,4},{9,5},{10,6},{11,7},{12,8},{13,9},{1... | collective-permute-start | bytes 3145736 | tf_op jit(solution)/shard_map/ppermute | solution.py:12
  483.6 46.3 %collective-permute-start.9 = (f32[2,256,512]{2,1,0:T(8,128)S(1)}, f32[2,256,512]{2,1,0:T(8,128)S(1)}, u32[]{:S(2)}, u32[]{:S(2)}) collective-permute-start(f32[2,256,512]{2,1,0:T(8,128)S(1)} %get-tuple-element.151), channel_id=1, source_target_pairs={{3,0},{4,1},{5,2},{6,3},{7,4},{8,5},{9,6},{10,7},{11,8},{12,9},{13... | collective-permute-start | bytes 3145736 | tf_op jit(solution)/shard_map/ppermute | solution.py:12
  532.2 41.8 %copy-start.1 = (bf16[768,512]{1,0:T(8,128)(2,1)S(1)}, bf16[768,512]{1,0:T(8,128)(2,1)}, u32[]{:S(2)}) copy-start(bf16[768,512]{1,0:T(8,128)(2,1)} %param.23) | copy-start | bytes 2359300
Sparse Core Ops, SparseCore 0:
  534.1 109.2 all-reduce.2
where the time goes:
time: 662 us; the launch traced here: 656 us
  starting transfers between devices  164 us (25%)
  waiting for transfers between devices  156 us (24%)
  loops' own time  129 us (19%)
  matrix products  76.7 us (12%)
  local copies, waits for them, and re-layouts  52.8 us (8%)
  blocking collectives  38.2 us (6%)
  other arithmetic  24.4 us (4%)
  between operations  14.2 us (2%)
    ppermute x16, starting transfers between devices, from_behind(): return lax.ppermute(block, axis, route)  164 us
    ppermute x16, waiting for transfers between devices, from_behind(): return lax.ppermute(block, axis, route)  88.3 us
    psum x1, waiting for transfers between devices, on_device(): lax.psum((local_self, local_neigh, local_bias), 'row')  68 us
    another operation x1, loops' own time, on_device(): lax.fori_loop(0, live_count, forward_block, jnp.zeros((trows, tile_size,...  64.6 us
    another operation x1, loops' own time, on_device(): lax.fori_loop(0, live_count, backward_block, jnp.zeros((span * trows, til...  64.4 us
    dot_general x14, matrix products, backward_block(): lax.dot_general(tiles[block], source, (((0,), (0,)), ((), ())), preferred...  39.6 us
    psum x1, blocking collectives, on_device(): lax.psum((local_self, local_neigh, local_bias), 'row')  38.2 us
    dot_general x14, matrix products, forward_block(): jnp.dot(tiles[block], source, preferred_element_type=jnp.float32)  26.6 us
  transfers between devices with their start and end apart: 17, of which 11 were waited for; matrix products, arithmetic and copies ran while one was open for 1% of the time, Pallas kernels for 0%

commit v1 on v0

v1 whole, which is shorter than its diff:
```python
import functools

import jax
import jax.numpy as jnp
from jax import lax
from jax.experimental import pallas as pl
from jax.experimental.pallas import tpu as pltpu
from jax.sharding import PartitionSpec as P

MESH = pl.DeviceIdType.MESH
F32 = jnp.float32
BF16 = jnp.bfloat16
CHUNKS = 4
NEAR = 9
TANH_SCALE = 0.7978845608028654
TANH_CUBE = 0.044715


def dot(a, b):
    return jnp.dot(a, b, preferred_element_type=F32)


def dot_nt(a, b):
    return lax.dot_general(a, b, (((1,), (1,)), ((), ())), preferred_element_type=F32)


def kernel(
    n_row,
    reduce_here,
    feat,
    degree,
    blist,
    bcount,
    tiles,
    w_self,
    w_neigh,
    bias,
    cot,
    act_out,
    gfeat_out,
    gself_out,
    gneigh_out,
    gbias_out,
    win,
    dense,
    dense_t,
    feat_t,
    acc,
    gpre_b,
    msg,
    lane_out,
    lane_in,
    net_out,
    net_in,
    gloc,
    tab,
    fsend,
    frecv,
    lsend,
    lrecv,
    nsend,
    nrecv,
    *red
):
    row = lax.axis_index("row")
    core = lax.rem(row, 2)
    chip = row // 2
    chips = n_row // 2
    side = lax.rem(chip, 2)
    sgn = 2 * side - 1

    def at(chip_off, c):
        return lax.rem(chip + chip_off + 4 * chips, chips) * 2 + c

    other = 1 - core
    partner = at(0, other)
    ypair = at(-sgn, core)
    zpos = at(2 * sgn, core)
    zneg = at(-2 * sgn, core)
    greet = [partner, ypair, zpos, zneg]
    if reduce_here:
        zline = [at(2 * j, core) for j in range(1, chips // 2)]
        greet = [partner, ypair] + zline

    def rc(src, dst, ssem, rsem, dev):
        return pltpu.make_async_remote_copy(
            src_ref=src,
            dst_ref=dst,
            send_sem=ssem,
            recv_sem=rsem,
            device_id={"row": dev},
            device_id_type=MESH,
        )

    barrier = pltpu.get_barrier_semaphore()
    for dev in greet:
        pl.semaphore_signal(barrier, inc=1, device_id={"row": dev}, device_id_type=MESH)
    pl.semaphore_wait(barrier, len(greet))

    nodes = feat.shape[0]
    tile = tiles.shape[1]
    step = nodes // CHUNKS

    def rows_of(ch):
        return pl.ds(pl.multiple_of(ch * step, step), step)

    def loop(count, body):
        def run(i, carry):
            body(i)
            return carry

        lax.fori_loop(0, count, run, 0)

    far = 3 + lax.rem(core + side, 2)
    own_sends = ((0, 3, zpos), (1, 4, zneg), (2, 2, ypair), (3, 1, partner))

    def fcopy(i, src, dst, ch, dev):
        rows = rows_of(ch)
        return rc(win.at[src, rows], win.at[dst, rows], fsend.at[i, ch], frecv.at[dst, ch], dev)

    def fwait(slot, ch):
        fcopy(0, slot, slot, ch, partner).wait_recv()

    def project(ch):
        rows = rows_of(ch)
        win[0, rows, :] = dot(feat[rows, :], w_neigh[...]).astype(BF16)
        for i, dst, dev in own_sends:
            fcopy(i, 0, dst, ch, dev).start()

    loop(CHUNKS, project)

    devs = (
        at(0, core),
        at(0, other),
        at(-sgn, core),
        at(-2 * sgn, core),
        at(2 * sgn, core),
        at(-sgn, other),
        at(2 * (2 * core - 1), other),
        at(sgn, core),
        at(sgn, other),
    )
    for b, dev in enumerate(devs):
        tab[b] = dev
    slots = tiles.shape[0]

    def densify(b):
        for t in range(2):
            column = tab[b] * 2 + t

            def seek(j, found):
                return jnp.maximum(found, jnp.where(blist[j, 1] == column, j, 0))

            slot = lax.fori_loop(0, slots, seek, 0)
            target = blist[slot, 0] - 2 * row
            live = slot < bcount[0]
            block = tiles[slot]
            flipped = block.T
            for r in range(2):
                take = jnp.logical_and(live, target == r)
                here = pl.ds(r * tile, tile)
                there = pl.ds(t * tile, tile)
                dense[b, here, there] = jnp.where(take, block, jnp.zeros_like(block))
                dense_t[b, there, here] = jnp.where(take, flipped, jnp.zeros_like(flipped))

    loop(NEAR, densify)

    def self_part(ch):
        rows = rows_of(ch)
        acc[rows, :] = dot(dense[0, rows, :], win[0])

    loop(CHUNKS, self_part)

    def add_block(b):
        def body(ch):
            rows = rows_of(ch)
            acc[rows, :] += dot(dense[b, rows, :], win[b])

        loop(CHUNKS, body)

    def relay(ch):
        fwait(3, ch)
        fcopy(4, 3, 7, ch, ypair).start()
        fwait(2, ch)
        fcopy(5, 2, 5, ch, partner).start()
        fwait(4, ch)
        fcopy(6, far, 6, ch, partner).start()

    loop(CHUNKS, relay)
    feat_t[...] = feat[...].T

    def arrive(b):
        loop(CHUNKS, lambda ch: fwait(b, ch))
        add_block(b)

    arrive(1)
    add_block(2)
    add_block(3)
    add_block(4)
    arrive(5)
    arrive(6)

    def relay_on(ch):
        fwait(7, ch)
        fcopy(7, 7, 8, ch, partner).start()

    loop(CHUNKS, relay_on)
    add_block(7)
    arrive(8)

    bias_rows = 8

    def activate(ch, bias_sum):
        rows = rows_of(ch)
        inverse = 1.0 / degree[rows, :].astype(F32)
        pre = dot(feat[rows, :], w_self[...]) + acc[rows, :] * inverse + bias[...]
        square = pre * pre
        t = jnp.tanh(TANH_SCALE * (pre + TANH_CUBE * (square * pre)))
        half = 0.5 * (1.0 + t)
        act_out[rows, :] = (pre * half).astype(BF16)
        slope = half + (0.5 * TANH_SCALE) * pre * (1.0 - t * t) * (1.0 + (3.0 * TANH_CUBE) * square)
        grad_pre = cot[rows, :].astype(F32) * slope
        gpre_b[rows, :] = grad_pre.astype(BF16)
        msg[rows, :] = (grad_pre * inverse).astype(BF16)
        return bias_sum + jnp.sum(
            grad_pre.reshape(step // bias_rows, bias_rows, grad_pre.shape[1]), axis=0
        )

    bias_sum = lax.fori_loop(0, CHUNKS, activate, jnp.zeros((bias_rows, acc.shape[1]), F32))

    def term(b, rows):
        return dot(dense_t[b, rows, :], msg[...])

    def lcopy(i, ch):
        rows = rows_of(ch)
        return rc(lane_out.at[i, rows], lane_in.at[i, rows], lsend.at[i, ch], lrecv.at[i, ch], partner)

    def ncopy(i, ch, dev):
        rows = rows_of(ch)
        return rc(net_out.at[i, rows], net_in.at[i, rows], nsend.at[i, ch], nrecv.at[i, ch], dev)

    def lane_term(i, b):
        def body(ch):
            rows = rows_of(ch)
            lane_out[i, rows, :] = term(b, rows).astype(BF16)
            lcopy(i, ch).start()

        return body

    loop(CHUNKS, lane_term(0, 8))
    loop(CHUNKS, lane_term(1, 6))

    def send_relay(ch):
        rows = rows_of(ch)
        mine = term(7, rows)
        lcopy(0, ch).wait_recv()
        net_out[0, rows, :] = (mine + lane_in[0, rows, :].astype(F32)).astype(BF16)
        ncopy(0, ch, ypair).start()

    loop(CHUNKS, send_relay)
    far_pos = (core != side).astype(F32)
    far_neg = 1.0 - far_pos

    def send_pos(ch):
        rows = rows_of(ch)
        mine = term(4, rows)
        lcopy(1, ch).wait_recv()
        net_out[1, rows, :] = (mine + far_pos * lane_in[1, rows, :].astype(F32)).astype(BF16)
        ncopy(1, ch, zpos).start()

    loop(CHUNKS, send_pos)
    loop(CHUNKS, lane_term(2, 5))

    def send_y(ch):
        rows = rows_of(ch)
        mine = term(2, rows)
        lcopy(2, ch).wait_recv()
        net_out[2, rows, :] = (mine + lane_in[2, rows, :].astype(F32)).astype(BF16)
        ncopy(2, ch, ypair).start()

    loop(CHUNKS, send_y)

    def send_neg(ch):
        rows = rows_of(ch)
        mine = term(3, rows) + far_neg * lane_in[1, rows, :].astype(F32)
        ncopy(0, ch, ypair).wait_recv()
        net_out[3, rows, :] = (mine + net_in[0, rows, :].astype(F32)).astype(BF16)
        ncopy(3, ch, zneg).start()

    loop(CHUNKS, send_neg)
    loop(CHUNKS, lane_term(3, 1))

    f_in = feat.shape[1]
    half_f, quarter_f = f_in // 2, f_in // 4
    f_step = f_in // CHUNKS

    def weight_grad(g, source):
        def body(i):
            rows = pl.ds(pl.multiple_of(i * f_step, f_step), f_step)
            gloc[g, rows, :] = dot(feat_t[rows, :], source[...])

        loop(CHUNKS, body)

    weight_grad(0, gpre_b)

    if reduce_here:
        (s1, r1, s2, r2, s3, r3, gath, b_out, b_in, gs, gr, bs, br) = red
        depth = chips // 2
        piece_f = quarter_f // depth
        z = chip // 2
        my_half = pl.multiple_of(core * half_f, half_f)
        not_half = pl.multiple_of(other * half_f, half_f)
        my_quarter = pl.multiple_of(my_half + side * quarter_f, quarter_f)
        not_quarter = pl.multiple_of(my_half + (1 - side) * quarter_f, quarter_f)
        my_piece = pl.multiple_of(my_quarter + z * piece_f, piece_f)
        far_z = [lax.rem(z + j, depth) for j in range(1, depth)]

        def c1(g):
            return rc(s1.at[g], r1.at[g], gs.at[g, 0], gr.at[g, 0], partner)

        def c2(g):
            return rc(s2.at[g], r2.at[g], gs.at[g, 1], gr.at[g, 1], ypair)

        def c3(g, j):
            return rc(
                s3.at[g, far_z[j]], r3.at[g, j], gs.at[g, 2 + j], gr.at[g, 2 + j], zline[j]
            )

        def c4(g, j, mine=True):
            z_of = z if mine else lax.rem(z + depth - 1 - j, depth)
            ref = gath.at[g, core, side, z_of]
            return rc(ref, ref, gs.at[g, 1 + depth + j], gr.at[g, 1 + depth + j], zline[j])

        last = 2 * depth

        def c5(g, mine=True):
            ref = gath.at[g, core, side if mine else 1 - side]
            return rc(ref, ref, gs.at[g, last], gr.at[g, last], ypair)

        def c6(g, mine=True):
            ref = gath.at[g, core if mine else other]
            return rc(ref, ref, gs.at[g, last + 1], gr.at[g, last + 1], partner)

        def stage1(g):
            s1[g] = gloc[g, pl.ds(not_half, half_f), :].astype(BF16)
            c1(g).start()

        def stage2(g):
            c1(g).wait_recv()
            skip = pl.multiple_of((1 - side) * quarter_f, quarter_f)
            s2[g] = (
                gloc[g, pl.ds(not_quarter, quarter_f), :]
                + r1[g, pl.ds(skip, quarter_f), :].astype(F32)
            ).astype(BF16)
            c2(g).start()

        def stage3(g):
            keep = pl.multiple_of(side * quarter_f, quarter_f)
            mine = (
                gloc[g, pl.ds(my_quarter, quarter_f), :]
                + r1[g, pl.ds(keep, quarter_f), :].astype(F32)
            )
            c2(g).wait_recv()
            mine = mine + r2[g].astype(F32)
            gloc[g, pl.ds(my_quarter, quarter_f), :] = mine
            s3[g] = mine.astype(BF16).reshape(s3.shape[1:])
            for j in range(depth - 1):
                c3(g, j).start()

        def stage4(g):
            total = gloc[g, pl.ds(my_piece, piece_f), :]
            for j in range(depth - 1):
                c3(g, j).wait_recv()
                total = total + r3[g, j].astype(F32)
            gath[g, core, side, z] = total.astype(BF16)
            for j in range(depth - 1):
                c4(g, j).start()

        def stage5(g):
            for j in range(depth - 1):
                c4(g, j, False).wait_recv()
            c5(g).start()

        def stage6(g):
            c5(g, False).wait_recv()
            c6(g).start()

        def stage7(g, out):
            c6(g, False).wait_recv()
            out[...] = gath[g].astype(F32).reshape(out.shape)

        def bcopy(i, src, dev):
            return rc(b_out.at[src], b_in.at[i], bs.at[i], br.at[i], dev)

        b_out[0] = bias_sum
        bcopy(0, 0, partner).start()
        stage1(0)
        bcopy(0, 0, partner).wait_recv()
        b_out[1] = b_out[0] + b_in[0]
        bcopy(1, 1, ypair).start()
        stage2(0)
        bcopy(1, 1, ypair).wait_recv()
        b_out[2] = b_out[1] + b_in[1]
        for j in range(depth - 1):
            bcopy(2 + j, 2, zline[j]).start()

    g_rows = nodes // CHUNKS

    def feature_grad(ch):
        rows = rows_of(ch)
        gfeat_out[rows, :] = dot_nt(gpre_b[rows, :], w_self[...]).astype(BF16)

    def gather_own(ch):
        rows = rows_of(ch)
        total = term(0, rows)
        lcopy(3, ch).wait_recv()
        total = total + lane_in[3, rows, :].astype(F32)
        ncopy(2, ch, ypair).wait_recv()
        total = total + net_in[2, rows, :].astype(F32)
        ncopy(1, ch, zpos).wait_recv()
        total = total + net_in[1, rows, :].astype(F32)
        ncopy(3, ch, zneg).wait_recv()
        total = total + net_in[3, rows, :].astype(F32)
        msg_back[rows, :] = total.astype(BF16)

    msg_back = win.at[0]
    if reduce_here:
        stage3(0)
        stage4(0)
    for i, src, dst in ((0, 0, 3), (1, 0, 4), (2, 0, 2), (3, 0, 1), (4, 3, 7), (5, 2, 5), (6, 3, 6), (7, 7, 8)):
        loop(CHUNKS, lambda ch, i=i, src=src, dst=dst: fcopy(i, src, dst, ch, partner).wait_send())
    loop(CHUNKS, gather_own)
    weight_grad(1, msg_back)
    if reduce_here:
        stage1(1)
        stage5(0)
        stage2(1)
        stage6(0)
        stage3(1)

    def feature_grad(ch):
        rows = rows_of(ch)
        gfeat_out[rows, :] = (
            dot_nt(gpre_b[rows, :], w_self[...]) + dot_nt(msg_back[rows, :], w_neigh[...])
        ).astype(BF16)

    loop(CHUNKS, feature_grad)
    if reduce_here:
        stage4(1)
        stage7(0, gself_out)
        total = b_out[2]
        for j in range(depth - 1):
            bcopy(2 + j, 2, zline[j]).wait_recv()
            total = total + b_in[2 + j]
        gbias_out[...] = jnp.sum(total, axis=0, keepdims=True)
        stage5(1)
        stage6(1)
        stage7(1, gneigh_out)
        for g in range(2):
            c1(g).wait_send()
            c2(g).wait_send()
            for j in range(depth - 1):
                c3(g, j).wait_send()
                c4(g, j).wait_send()
            c5(g).wait_send()
            c6(g).wait_send()
        bcopy(0, 0, partner).wait_send()
        bcopy(1, 1, ypair).wait_send()
        for j in range(depth - 1):
            bcopy(2 + j, 2, zline[j]).wait_send()
    else:
        gself_out[...] = gloc[0]
        gneigh_out[...] = gloc[1]
        gbias_out[...] = jnp.sum(bias_sum, axis=0, keepdims=True)

    def drain(ch):
        for i in range(4):
            lcopy(i, ch).wait_send()
        for i, dev in enumerate((ypair, zpos, ypair, zneg)):
            ncopy(i, ch, dev).wait_send()

    loop(CHUNKS, drain)


def on_device(
    features, degree, block_list, block_count, tiles, self_weight, neigh_weight, bias, cotangent
):
    nodes, f_in = features.shape
    hid = neigh_weight.shape[1]
    n_row = lax.axis_size("row")
    depth = n_row // 4
    reduce_here = False
    vmem = pl.BlockSpec(memory_space=pltpu.VMEM)
    smem = pl.BlockSpec(memory_space=pltpu.SMEM)
    dma = pltpu.SemaphoreType.DMA
    block = (nodes, hid)
    scratch = [
        pltpu.VMEM((NEAR,) + block, BF16),
        pltpu.VMEM((NEAR, nodes, nodes), BF16),
        pltpu.VMEM((NEAR, nodes, nodes), BF16),
        pltpu.VMEM((f_in, nodes), BF16),
        pltpu.VMEM(block, F32),
        pltpu.VMEM(block, BF16),
        pltpu.VMEM(block, BF16),
        pltpu.VMEM((4,) + block, BF16),
        pltpu.VMEM((4,) + block, BF16),
        pltpu.VMEM((4,) + block, BF16),
        pltpu.VMEM((4,) + block, BF16),
        pltpu.VMEM((2, f_in, hid), F32),
        pltpu.SMEM((NEAR,), jnp.int32),
        dma((8, CHUNKS)),
        dma((NEAR, CHUNKS)),
        dma((4, CHUNKS)),
        dma((4, CHUNKS)),
        dma((4, CHUNKS)),
        dma((4, CHUNKS)),
    ]
    if reduce_here:
        half, quarter = f_in // 2, f_in // 4
        scratch += [
            pltpu.VMEM((2, half, hid), BF16),
            pltpu.VMEM((2, half, hid), BF16),
            pltpu.VMEM((2, quarter, hid), BF16),
            pltpu.VMEM((2, quarter, hid), BF16),
            pltpu.VMEM((2, depth, quarter // depth, hid), BF16),
            pltpu.VMEM((2, depth - 1, quarter // depth, hid), BF16),
            pltpu.VMEM((2, 2, 2, depth, quarter // depth, hid), BF16),
            pltpu.VMEM((3, 8, hid), F32),
            pltpu.VMEM((1 + depth, 8, hid), F32),
            dma((2, 2 * depth + 2)),
            dma((2, 2 * depth + 2)),
            dma((1 + depth,)),
            dma((1 + depth,)),
        ]
    act, gfeat, gself, gneigh, gbias = pl.pallas_call(
        functools.partial(kernel, n_row, reduce_here),
        out_shape=(
            jax.ShapeDtypeStruct(block, BF16),
            jax.ShapeDtypeStruct((nodes, f_in), BF16),
            jax.ShapeDtypeStruct((f_in, hid), F32),
            jax.ShapeDtypeStruct((f_in, hid), F32),
            jax.ShapeDtypeStruct((1, hid), F32),
        ),
        in_specs=[vmem, vmem, smem, smem, vmem, vmem, vmem, vmem, vmem],
        out_specs=(vmem,) * 5,
        scratch_shapes=scratch,
        compiler_params=pltpu.CompilerParams(
            collective_id=0, has_side_effects=True, vmem_limit_bytes=60 * 1024 * 1024
        ),
    )(
        features,
        degree.reshape(nodes, 1),
        block_list,
        block_count,
        tiles,
        self_weight,
        neigh_weight,
        bias.reshape(1, hid),
        cotangent,
    )
    gbias = gbias.reshape(hid)
    if not reduce_here:
        gself, gneigh, gbias = lax.psum((gself, gneigh, gbias), "row")
    return act, gfeat, gself, gneigh, gbias


def solution(mesh):
    return jax.shard_map(
        on_device,
        mesh=mesh,
        in_specs=(
            P(("grp", "row"), None),
            P(("grp", "row")),
            P(("grp", "row"), None),
            P(("grp", "row")),
            P(("grp", "row"), None, None),
            P(),
            P(),
            P(),
            P(("grp", "row"), None),
        ),
        out_specs=(
            P(("grp", "row"), None),
            P(("grp", "row"), None),
            P("grp", None),
            P("grp", None),
            P("grp"),
        ),
        check_vma=False,
    )
```

time: 662 us -> 204 us (0.31)
  starting transfers between devices: 164 us -> 0.04 us
  loops' own time: 129 us -> 0 us
  waiting for transfers between devices: 156 us -> 71.3 us
  Pallas kernels: 0 us -> 76.8 us
  matrix products: 76.7 us -> 0 us
  local copies, waits for them, and re-layouts: 52.8 us -> 8.32 us
  other arithmetic: 24.4 us -> 0 us
  blocking collectives: 38.2 us -> 30.3 us
    ppermute x16 -> x0, starting transfers between devices: 164 us -> none  [from_behind(): return lax.ppermute(block, axis, route)]
    another operation x2 -> x0, loops' own time: 129 us -> none  [the longest x1 64.6 us: on_device(): lax.fori_loop(0, live_count, forward_block, jnp.zeros((trows, tile_size,...]
    ppermute x16 -> x0, waiting for transfers between devices: 88.3 us -> none  [from_behind(): return lax.ppermute(block, axis, route)]
    pallas_call x0 -> x1, Pallas kernels: none -> 76.8 us  [on_device(): pl.pallas_call(functools.partial(kernel, n_row, reduce_here), out_shape=(...]
    dot_general x34 -> x0, matrix products: 76.7 us -> none  [the longest x14 39.6 us: backward_block(): lax.dot_general(tiles[block], source, (((0,), (0,)), ((), ())), preferred...]
    dynamic_slice x56 -> x0, local copies, waits for them, and re-layouts: 32.9 us -> none  [the longest x14 8.25 us: forward_block(): return gathered.at[row_slot[block]].add(partial_value)]
    another operation x28 -> x0, other arithmetic: 19.9 us -> none
    psum x1, blocking collectives: 38.2 us -> 30.3 us  [on_device(): gself, gneigh, gbias = lax.psum((gself, gneigh, gbias), 'row')]
  transfers between devices with their start and end apart: 17 -> 1, of which waited for: 11 -> 1; matrix products, arithmetic and copies ran while one was open for 1% -> 0% of each run, Pallas kernels for 0% -> 0%
where the time goes in v1:
time: 204 us; the launch traced here: 201 us
  Pallas kernels  76.8 us (38%)
  waiting for transfers between devices  71.3 us (35%)
  blocking collectives  30.3 us (15%)
  between operations  14.7 us (7%)
  local copies, waits for them, and re-layouts  8.32 us (4%)
    pallas_call x1, Pallas kernels, on_device(): pl.pallas_call(functools.partial(kernel, n_row, reduce_here), out_shape=(...  76.8 us
    psum x1, waiting for transfers between devices, on_device(): gself, gneigh, gbias = lax.psum((gself, gneigh, gbias), 'row')  71.2 us
    psum x1, blocking collectives, on_device(): gself, gneigh, gbias = lax.psum((gself, gneigh, gbias), 'row')  30.3 us
    unnamed x15, local copies, waits for them, and re-layouts  6.79 us
  transfers between devices with their start and end apart: 1, of which 1 were waited for; matrix products, arithmetic and copies ran while one was open for 0% of the time, Pallas kernels for 0%

profile of v1, /device:TPU:1, one launch (start us, length us, event | category | flops | bytes accessed | tf_op | source)
XLA Modules:
  0.0 201.4 jit_solution(11157918158740094539)
XLA Ops:
  7.2 0.0 all-reduce.3.cloned.1.call-start
  7.9 1.4 copy.16.blist
  9.2 1.5 copy.15.degree
  10.8 76.8 %shard_map.128 = (bf16[512,512]{1,0:T(8,128)(2,1)}, bf16[512,768]{1,0:T(8,128)(2,1)}, f32[768,512]{1,0:T(8,128)}, f32[768,512]{1,0:T(8,128)}, f32[1,512]{1,0:T(1,128)}) custom-call(bf16[512,768]{1,0:T(8,128)(2,1)} %feat.1, s32[512,1]{1,0:T(8,128)} %copy.15.degree, s32[18,2]{1,0:T(8,128)} %copy.16.blist, s32[1]{0:T(128)S(6)} %copy.23.bcount, ...), custom_call_target="tpu_custom_call" | custom-call | tf_op jit(solution)/shard_map/pallas_call | solution.py:535
  87.5 0.0 copy-start.4
  87.5 0.0 copy-start.3
  87.5 0.0 copy-start.2
  87.6 0.0 all-reduce.3.cloned.1.call-update
  87.6 0.6 copy-done.4
  88.2 30.3 %psum.23 = f32[512]{0:T(512)} all-reduce(f32[512]{0:T(512)S(1)} %bitcast.5), channel_id=1, replica_groups=mesh['grp'=2,'row'=16] {'row'}, use_global_device_ids=true, to_apply=%region_2.0 | all-reduce | flops 512 | bytes 4096 | tf_op jit(solution)/shard_map/psum | solution.py:563
  118.5 71.2 %all-reduce.3.cloned.1.call-done = (f32[768,512]{1,0:T(8,128)}, f32[768,512]{1,0:T(8,128)}) async-done(((f32[768,512]{1,0:T(8,128)}, f32[768,512]{1,0:T(8,128)}), (f32[768,512]{1,0:T(8,128)}, f32[768,512]{1,0:T(8,128)})) %all-reduce.3.cloned.1.call-update) | async-done | bytes 3145744 | tf_op jit(solution)/shard_map/psum | solution.py:563
  189.8 0.0 copy-start.1
  189.8 0.0 copy-done.3
  189.8 0.8 copy.24
  190.6 0.0 copy-done.2
  190.6 0.9 copy.25
  191.5 0.0 copy-done.1
  191.5 0.0 copy-start
  191.5 1.1 copy.26
  192.6 0.8 copy-done
  193.4 1.1 copy.27
Async XLA Ops:
  7.2 182.6 %all-reduce.3.cloned.1.call-start = ((), (), s32[]{:S(2)}) async-start(), calls=%async_computation | async-start | bytes 6291456 | tf_op jit(solution)/shard_map/psum | solution.py:563
  87.5 0.7 copy-start.4
  87.5 102.3 %copy-start.3 = (bf16[512,512]{1,0:T(8,128)(2,1)S(1)}, bf16[512,512]{1,0:T(8,128)(2,1)}, u32[]{:S(2)}) copy-start(bf16[512,512]{1,0:T(8,128)(2,1)} %get-tuple-element.22) | copy-start | bytes 1572868
  87.5 103.0 %copy-start.2 = (bf16[512,768]{1,0:T(8,128)(2,1)S(1)}, bf16[512,768]{1,0:T(8,128)(2,1)}, u32[]{:S(2)}) copy-start(bf16[512,768]{1,0:T(8,128)(2,1)} %get-tuple-element.23) | copy-start | bytes 2359300
  189.8 1.7 copy-start.1
  191.5 2.0 copy-start
Sparse Core Ops, SparseCore 0:
  87.7 102.0 all-reduce.2

commit v2 on v1

--- a/solution.py
+++ b/solution.py
@@ -323,47 +323,52 @@
 
         def c3(g, j):
             return rc(
-                s3.at[g, far_z[j]], r3.at[g, j], gs.at[g, 2 + j], gr.at[g, 2 + j], zline[j]
+                s3.at[g, j], r3.at[g, j], gs.at[g, 2 + j], gr.at[g, 2 + j], zline[j]
             )
 
-        def c4(g, j, mine=True):
-            z_of = z if mine else lax.rem(z + depth - 1 - j, depth)
-            ref = gath.at[g, core, side, z_of]
-            return rc(ref, ref, gs.at[g, 1 + depth + j], gr.at[g, 1 + depth + j], zline[j])
+        def c4(g, j):
+            return rc(
+                gath.at[g, 0, 0, 0],
+                gath.at[g, 0, 0, j + 1],
+                gs.at[g, 1 + depth + j],
+                gr.at[g, 1 + depth + j],
+                zline[j],
+            )
 
         last = 2 * depth
 
-        def c5(g, mine=True):
-            ref = gath.at[g, core, side if mine else 1 - side]
-            return rc(ref, ref, gs.at[g, last], gr.at[g, last], ypair)
-
-        def c6(g, mine=True):
-            ref = gath.at[g, core if mine else other]
-            return rc(ref, ref, gs.at[g, last + 1], gr.at[g, last + 1], partner)
+        def c5(g):
+            return rc(gath.at[g, 0, 0], gath.at[g, 0, 1], gs.at[g, last], gr.at[g, last], ypair)
+
+        def c6(g):
+            return rc(gath.at[g, 0], gath.at[g, 1], gs.at[g, last + 1], gr.at[g, last + 1], partner)
 
         def stage1(g):
-            s1[g] = gloc[g, pl.ds(not_half, half_f), :].astype(BF16)
+            for a in range(2):
+                start = not_half + (side if a == 0 else 1 - side) * quarter_f
+                rows = pl.ds(pl.multiple_of(start, quarter_f), quarter_f)
+                s1[g, a] = gloc[g, rows, :].astype(BF16)
             c1(g).start()
 
         def stage2(g):
             c1(g).wait_recv()
-            skip = pl.multiple_of((1 - side) * quarter_f, quarter_f)
             s2[g] = (
                 gloc[g, pl.ds(not_quarter, quarter_f), :]
-                + r1[g, pl.ds(skip, quarter_f), :].astype(F32)
+                + r1[g, 1].astype(F32)
             ).astype(BF16)
             c2(g).start()
 
         def stage3(g):
-            keep = pl.multiple_of(side * quarter_f, quarter_f)
             mine = (
                 gloc[g, pl.ds(my_quarter, quarter_f), :]
-                + r1[g, pl.ds(keep, quarter_f), :].astype(F32)
+                + r1[g, 0].astype(F32)
             )
             c2(g).wait_recv()
             mine = mine + r2[g].astype(F32)
             gloc[g, pl.ds(my_quarter, quarter_f), :] = mine
-            s3[g] = mine.astype(BF16).reshape(s3.shape[1:])
+            for j in range(depth - 1):
+                start = pl.multiple_of(my_quarter + far_z[j] * piece_f, piece_f)
+                s3[g, j] = gloc[g, pl.ds(start, piece_f), :].astype(BF16)
             for j in range(depth - 1):
                 c3(g, j).start()
 
@@ -372,22 +377,29 @@
             for j in range(depth - 1):
                 c3(g, j).wait_recv()
                 total = total + r3[g, j].astype(F32)
-            gath[g, core, side, z] = total.astype(BF16)
+            gath[g, 0, 0, 0] = total.astype(BF16)
             for j in range(depth - 1):
                 c4(g, j).start()
 
         def stage5(g):
             for j in range(depth - 1):
-                c4(g, j, False).wait_recv()
+                c4(g, j).wait_recv()
             c5(g).start()
 
         def stage6(g):
-            c5(g, False).wait_recv()
+            c5(g).wait_recv()
             c6(g).start()
 
         def stage7(g, out):
-            c6(g, False).wait_recv()
-            out[...] = gath[g].astype(F32).reshape(out.shape)
+            c6(g).wait_recv()
+            for a in range(2):
+                for b in range(2):
+                    base = (core if a == 0 else other) * half_f
+                    base = base + (side if b == 0 else 1 - side) * quarter_f
+                    for j in range(depth):
+                        start = base + lax.rem(z + depth - j, depth) * piece_f
+                        rows = pl.ds(pl.multiple_of(start, piece_f), piece_f)
+                        out[rows, :] = gath[g, a, b, j].astype(F32)
 
         def bcopy(i, src, dev):
             return rc(b_out.at[src], b_in.at[i], bs.at[i], br.at[i], dev)
@@ -489,7 +501,7 @@
     hid = neigh_weight.shape[1]
     n_row = lax.axis_size("row")
     depth = n_row // 4
-    reduce_here = False
+    reduce_here = f_in % (4 * depth * 16) == 0 and depth >= 3 and depth <= 4
     vmem = pl.BlockSpec(memory_space=pltpu.VMEM)
     smem = pl.BlockSpec(memory_space=pltpu.SMEM)
     dma = pltpu.SemaphoreType.DMA
@@ -516,13 +528,13 @@
         dma((4, CHUNKS)),
     ]
     if reduce_here:
-        half, quarter = f_in // 2, f_in // 4
+        quarter = f_in // 4
         scratch += [
-            pltpu.VMEM((2, half, hid), BF16),
-            pltpu.VMEM((2, half, hid), BF16),
+            pltpu.VMEM((2, 2, quarter, hid), BF16),
+            pltpu.VMEM((2, 2, quarter, hid), BF16),
             pltpu.VMEM((2, quarter, hid), BF16),
             pltpu.VMEM((2, quarter, hid), BF16),
-            pltpu.VMEM((2, depth, quarter // depth, hid), BF16),
+            pltpu.VMEM((2, depth - 1, quarter // depth, hid), BF16),
             pltpu.VMEM((2, depth - 1, quarter // depth, hid), BF16),
             pltpu.VMEM((2, 2, 2, depth, quarter // depth, hid), BF16),
             pltpu.VMEM((3, 8, hid), F32),

time: 204 us -> 128 us (0.63); the launches traced: 201 us -> 128 us
  waiting for transfers between devices: 71.3 us -> 0 us
  Pallas kernels: 76.8 us -> 116 us
  blocking collectives: 30.3 us -> 0 us
  between operations: 14.7 us -> 1.3 us
  local copies, waits for them, and re-layouts: 8.32 us -> 10.6 us
    psum x1 -> x0, waiting for transfers between devices: 71.2 us -> none  [on_device(): gself, gneigh, gbias = lax.psum((gself, gneigh, gbias), 'row')]
    pallas_call x1, Pallas kernels: 76.8 us -> 116 us  [on_device(): pl.pallas_call(functools.partial(kernel, n_row, reduce_here), out_shape=(...]
    psum x1 -> x0, blocking collectives: 30.3 us -> none  [on_device(): gself, gneigh, gbias = lax.psum((gself, gneigh, gbias), 'row')]
    unnamed x15 -> x12, local copies, waits for them, and re-layouts: 6.79 us -> 9.12 us
  transfers between devices with their start and end apart: 1 -> 0, of which waited for: 1 -> 0; matrix products, arithmetic and copies ran while one was open for 0% -> 0% of each run, Pallas kernels for 0% -> 0%
where the time goes in v2:
time: 128 us
  Pallas kernels  116 us (91%)
  local copies, waits for them, and re-layouts  10.6 us (8%)
  between operations  1.3 us (1%)
    pallas_call x1, Pallas kernels, on_device(): pl.pallas_call(functools.partial(kernel, n_row, reduce_here), out_shape=(...  116 us
    unnamed x12, local copies, waits for them, and re-layouts  9.12 us

profile of v2, /device:TPU:1, one launch (start us, length us, event | category | flops | bytes accessed | tf_op | source)
XLA Modules:
  0.0 127.9 jit_solution(5687720253697106692)
XLA Ops:
  1.3 1.4 %copy.16.blist = s32[18,2]{1,0:T(8,128)} copy(s32[18,2]{0,1:T(2,128)} %param.11) | data formatting | bytes 288 | tf_op args[2]
  2.6 1.5 %copy.15.degree = s32[512,1]{1,0:T(8,128)} copy(s32[512,1]{0,1:T(1,128)} %bitcast.3) | data formatting | bytes 4096 | tf_op jit(solution)/shard_map/reshape | solution.py:564
  4.2 115.9 %shard_map.128 = (bf16[512,512]{1,0:T(8,128)(2,1)}, bf16[512,768]{1,0:T(8,128)(2,1)}, f32[768,512]{1,0:T(8,128)}, f32[768,512]{1,0:T(8,128)}, f32[1,512]{1,0:T(1,128)}) custom-call(bf16[512,768]{1,0:T(8,128)(2,1)} %feat.1, s32[512,1]{1,0:T(8,128)} %copy.15.degree, s32[18,2]{1,0:T(8,128)} %copy.16.blist, s32[1]{0:T(128)S(6)} %copy.22.bcount, ...), custom_call_target="tpu_custom_call" | custom-call | tf_op jit(solution)/shard_map/pallas_call | solution.py:547
  120.1 0.0 copy-start.1
  120.1 2.0 %copy.23 = bf16[512,512]{1,0:T(8,128)(2,1)} copy(bf16[512,512]{1,0:T(8,128)(2,1)} %get-tuple-element.20) | data formatting | bytes 1048576
  122.1 2.1 %copy.24 = bf16[512,768]{1,0:T(8,128)(2,1)} copy(bf16[512,768]{1,0:T(8,128)(2,1)} %get-tuple-element.21) | data formatting | bytes 1572864
  124.2 0.0 copy-done.1
  124.2 0.0 copy-start
  124.2 1.1 copy.25
  125.3 0.8 copy-done
  126.2 0.0 copy-start.2
  126.2 1.1 copy.26
  127.3 0.0 copy-done.2
  127.3 0.6 copy.27
Async XLA Ops:
  120.1 4.1 %copy-start.1 = (f32[768,512]{1,0:T(8,128)S(1)}, f32[768,512]{1,0:T(8,128)}, u32[]{:S(2)}) copy-start(f32[768,512]{1,0:T(8,128)} %get-tuple-element.22) | copy-start | bytes 4718596
  124.2 2.0 %copy-start = (f32[768,512]{1,0:T(8,128)S(1)}, f32[768,512]{1,0:T(8,128)}, u32[]{:S(2)}) copy-start(f32[768,512]{1,0:T(8,128)} %get-tuple-element.23) | copy-start | bytes 4718596
  126.2 1.1 copy-start.2

commit v3 on v2

--- a/solution.py
+++ b/solution.py
@@ -163,14 +163,6 @@
                 dense[b, here, there] = jnp.where(take, block, jnp.zeros_like(block))
                 dense_t[b, there, here] = jnp.where(take, flipped, jnp.zeros_like(flipped))
 
-    loop(NEAR, densify)
-
-    def self_part(ch):
-        rows = rows_of(ch)
-        acc[rows, :] = dot(dense[0, rows, :], win[0])
-
-    loop(CHUNKS, self_part)
-
     def add_block(b):
         def body(ch):
             rows = rows_of(ch)
@@ -186,7 +178,20 @@
         fwait(4, ch)
         fcopy(6, far, 6, ch, partner).start()
 
-    loop(CHUNKS, relay)
+    def densify_and_relay(ch):
+        densify(2 * ch)
+        densify(2 * ch + 1)
+        relay(ch)
+
+    loop(CHUNKS, densify_and_relay)
+    densify(NEAR - 1)
+
+    def self_part(ch):
+        rows = rows_of(ch)
+        acc[rows, :] = dot(dense[0, rows, :], win[0])
+
+    loop(CHUNKS, self_part)
+
     feat_t[...] = feat[...].T
 
     def arrive(b):
@@ -212,7 +217,8 @@
 
     def activate(ch, bias_sum):
         rows = rows_of(ch)
-        inverse = 1.0 / degree[rows, :].astype(F32)
+        per_node = 1.0 / degree[pl.ds(ch, 1), :].astype(F32)
+        inverse = jnp.broadcast_to(per_node, (step, step)).T[:, :1]
         pre = dot(feat[rows, :], w_self[...]) + acc[rows, :] * inverse + bias[...]
         square = pre * pre
         t = jnp.tanh(TANH_SCALE * (pre + TANH_CUBE * (square * pre)))
@@ -294,16 +300,9 @@
     half_f, quarter_f = f_in // 2, f_in // 4
     f_step = f_in // CHUNKS
 
-    def weight_grad(g, source):
-        def body(i):
-            rows = pl.ds(pl.multiple_of(i * f_step, f_step), f_step)
-            gloc[g, rows, :] = dot(feat_t[rows, :], source[...])
-
-        loop(CHUNKS, body)
-
-    weight_grad(0, gpre_b)
-
-    if reduce_here:
+    width = gloc.shape[2]
+
+    def reduce_stages():
         (s1, r1, s2, r2, s3, r3, gath, b_out, b_in, gs, gr, bs, br) = red
         depth = chips // 2
         piece_f = quarter_f // depth
@@ -390,7 +389,9 @@
             c5(g).wait_recv()
             c6(g).start()
 
-        def stage7(g, out):
+        def stage7(g):
+            out = gself_out if g < 2 else gneigh_out
+            cols = pl.ds(g % 2 * width, width)
             c6(g).wait_recv()
             for a in range(2):
                 for b in range(2):
@@ -399,28 +400,67 @@
                     for j in range(depth):
                         start = base + lax.rem(z + depth - j, depth) * piece_f
                         rows = pl.ds(pl.multiple_of(start, piece_f), piece_f)
-                        out[rows, :] = gath[g, a, b, j].astype(F32)
+                        out[rows, cols] = gath[g, a, b, j]
 
         def bcopy(i, src, dev):
             return rc(b_out.at[src], b_in.at[i], bs.at[i], br.at[i], dev)
 
-        b_out[0] = bias_sum
-        bcopy(0, 0, partner).start()
+        def bias_start():
+            b_out[0] = bias_sum
+            bcopy(0, 0, partner).start()
+            bcopy(0, 0, partner).wait_recv()
+            b_out[1] = b_out[0] + b_in[0]
+            bcopy(1, 1, ypair).start()
+            bcopy(1, 1, ypair).wait_recv()
+            b_out[2] = b_out[1] + b_in[1]
+            for j in range(depth - 1):
+                bcopy(2 + j, 2, zline[j]).start()
+
+        def bias_end():
+            total = b_out[2]
+            for j in range(depth - 1):
+                bcopy(2 + j, 2, zline[j]).wait_recv()
+                total = total + b_in[2 + j]
+            gbias_out[...] = jnp.sum(total, axis=0, keepdims=True)
+
+        def settle():
+            for g in range(4):
+                c1(g).wait_send()
+                c2(g).wait_send()
+                for j in range(depth - 1):
+                    c3(g, j).wait_send()
+                    c4(g, j).wait_send()
+                c5(g).wait_send()
+                c6(g).wait_send()
+            bcopy(0, 0, partner).wait_send()
+            bcopy(1, 1, ypair).wait_send()
+            for j in range(depth - 1):
+                bcopy(2 + j, 2, zline[j]).wait_send()
+
+        return (
+            stage1, stage2, stage3, stage4, stage5, stage6, stage7, bias_start, bias_end, settle
+        )
+
+    def weight_grad(u, source):
+        cols = pl.ds(u % 2 * width, width)
+
+        def body(i):
+            rows = pl.ds(pl.multiple_of(i * f_step, f_step), f_step)
+            gloc[u, rows, :] = dot(feat_t[rows, :], source[:, cols])
+
+        loop(CHUNKS, body)
+
+    weight_grad(0, gpre_b)
+    if reduce_here:
+        stages = reduce_stages()
+        stage1, stage2, stage3, stage4, stage5, stage6, stage7, bias_start, bias_end, settle = stages
         stage1(0)
-        bcopy(0, 0, partner).wait_recv()
-        b_out[1] = b_out[0] + b_in[0]
-        bcopy(1, 1, ypair).start()
+    weight_grad(1, gpre_b)
+    if reduce_here:
+        stage1(1)
+        bias_start()
         stage2(0)
-        bcopy(1, 1, ypair).wait_recv()
-        b_out[2] = b_out[1] + b_in[1]
-        for j in range(depth - 1):
-            bcopy(2 + j, 2, zline[j]).start()
-
-    g_rows = nodes // CHUNKS
-
-    def feature_grad(ch):
-        rows = rows_of(ch)
-        gfeat_out[rows, :] = dot_nt(gpre_b[rows, :], w_self[...]).astype(BF16)
+        stage2(1)
 
     def gather_own(ch):
         rows = rows_of(ch)
@@ -438,17 +478,10 @@
     msg_back = win.at[0]
     if reduce_here:
         stage3(0)
-        stage4(0)
+        stage3(1)
     for i, src, dst in ((0, 0, 3), (1, 0, 4), (2, 0, 2), (3, 0, 1), (4, 3, 7), (5, 2, 5), (6, 3, 6), (7, 7, 8)):
         loop(CHUNKS, lambda ch, i=i, src=src, dst=dst: fcopy(i, src, dst, ch, partner).wait_send())
     loop(CHUNKS, gather_own)
-    weight_grad(1, msg_back)
-    if reduce_here:
-        stage1(1)
-        stage5(0)
-        stage2(1)
-        stage6(0)
-        stage3(1)
 
     def feature_grad(ch):
         rows = rows_of(ch)
@@ -456,33 +489,41 @@
             dot_nt(gpre_b[rows, :], w_self[...]) + dot_nt(msg_back[rows, :], w_neigh[...])
         ).astype(BF16)
 
+    weight_grad(2, msg_back)
+    if reduce_here:
+        stage1(2)
+    weight_grad(3, msg_back)
+    if reduce_here:
+        stage1(3)
+        stage2(2)
+        stage4(0)
+        stage2(3)
+        stage4(1)
+        stage3(2)
+        stage5(0)
+        stage3(3)
+        stage5(1)
+        stage6(0)
+        stage4(2)
+        stage6(1)
+        stage4(3)
+        stage5(2)
+        stage5(3)
     loop(CHUNKS, feature_grad)
     if reduce_here:
-        stage4(1)
-        stage7(0, gself_out)
-        total = b_out[2]
-        for j in range(depth - 1):
-            bcopy(2 + j, 2, zline[j]).wait_recv()
-            total = total + b_in[2 + j]
-        gbias_out[...] = jnp.sum(total, axis=0, keepdims=True)
-        stage5(1)
-        stage6(1)
-        stage7(1, gneigh_out)
-        for g in range(2):
-            c1(g).wait_send()
-            c2(g).wait_send()
-            for j in range(depth - 1):
-                c3(g, j).wait_send()
-                c4(g, j).wait_send()
-            c5(g).wait_send()
-            c6(g).wait_send()
-        bcopy(0, 0, partner).wait_send()
-        bcopy(1, 1, ypair).wait_send()
-        for j in range(depth - 1):
-            bcopy(2 + j, 2, zline[j]).wait_send()
+        stage6(2)
+        stage6(3)
+        stage7(0)
+        stage7(1)
+        bias_end()
+        stage7(2)
+        stage7(3)
+        settle()
     else:
-        gself_out[...] = gloc[0]
-        gneigh_out[...] = gloc[1]
+        for u in range(4):
+            cols = pl.ds(u % 2 * width, width)
+            out = gself_out if u < 2 else gneigh_out
+            out[:, cols] = gloc[u]
         gbias_out[...] = jnp.sum(bias_sum, axis=0, keepdims=True)
 
     def drain(ch):
@@ -518,7 +559,7 @@
         pltpu.VMEM((4,) + block, BF16),
         pltpu.VMEM((4,) + block, BF16),
         pltpu.VMEM((4,) + block, BF16),
-        pltpu.VMEM((2, f_in, hid), F32),
+        pltpu.VMEM((4, f_in, hid // 2), F32),
         pltpu.SMEM((NEAR,), jnp.int32),
         dma((8, CHUNKS)),
         dma((NEAR, CHUNKS)),
@@ -528,19 +569,19 @@
         dma((4, CHUNKS)),
     ]
     if reduce_here:
-        quarter = f_in // 4
+        quarter, wide = f_in // 4, hid // 2
         scratch += [
-            pltpu.VMEM((2, 2, quarter, hid), BF16),
-            pltpu.VMEM((2, 2, quarter, hid), BF16),
-            pltpu.VMEM((2, quarter, hid), BF16),
-            pltpu.VMEM((2, quarter, hid), BF16),
-            pltpu.VMEM((2, depth - 1, quarter // depth, hid), BF16),
-            pltpu.VMEM((2, depth - 1, quarter // depth, hid), BF16),
-            pltpu.VMEM((2, 2, 2, depth, quarter // depth, hid), BF16),
+            pltpu.VMEM((4, 2, quarter, wide), BF16),
+            pltpu.VMEM((4, 2, quarter, wide), BF16),
+            pltpu.VMEM((4, quarter, wide), BF16),
+            pltpu.VMEM((4, quarter, wide), BF16),
+            pltpu.VMEM((4, depth - 1, quarter // depth, wide), BF16),
+            pltpu.VMEM((4, depth - 1, quarter // depth, wide), BF16),
+            pltpu.VMEM((4, 2, 2, depth, quarter // depth, wide), BF16),
             pltpu.VMEM((3, 8, hid), F32),
             pltpu.VMEM((1 + depth, 8, hid), F32),
-            dma((2, 2 * depth + 2)),
-            dma((2, 2 * depth + 2)),
+            dma((4, 2 * depth + 2)),
+            dma((4, 2 * depth + 2)),
             dma((1 + depth,)),
             dma((1 + depth,)),
         ]
@@ -549,8 +590,8 @@
         out_shape=(
             jax.ShapeDtypeStruct(block, BF16),
             jax.ShapeDtypeStruct((nodes, f_in), BF16),
-            jax.ShapeDtypeStruct((f_in, hid), F32),
-            jax.ShapeDtypeStruct((f_in, hid), F32),
+            jax.ShapeDtypeStruct((f_in, hid), BF16 if reduce_here else F32),
+            jax.ShapeDtypeStruct((f_in, hid), BF16 if reduce_here else F32),
             jax.ShapeDtypeStruct((1, hid), F32),
         ),
         in_specs=[vmem, vmem, smem, smem, vmem, vmem, vmem, vmem, vmem],
@@ -561,7 +602,7 @@
         ),
     )(
         features,
-        degree.reshape(nodes, 1),
+        degree.reshape(CHUNKS, nodes // CHUNKS),
         block_list,
         block_count,
         tiles,
@@ -571,6 +612,7 @@
         cotangent,
     )
     gbias = gbias.reshape(hid)
+    gself, gneigh = gself.astype(F32), gneigh.astype(F32)
     if not reduce_here:
         gself, gneigh, gbias = lax.psum((gself, gneigh, gbias), "row")
     return act, gfeat, gself, gneigh, gbias

time: 128 us -> 113 us (0.88)
  Pallas kernels: 116 us -> 104 us
  local copies, waits for them, and re-layouts: 10.6 us -> 3.63 us
  other arithmetic: 0 us -> 3.92 us
    pallas_call x1, Pallas kernels: 116 us -> 104 us  [on_device(): pl.pallas_call(functools.partial(kernel, n_row, reduce_here), out_shape=(...]
    unnamed x12, local copies, waits for them, and re-layouts: 9.12 us -> 3.63 us
    convert_element_type x0 -> x2, other arithmetic: none -> 3.92 us  [on_device(): gself, gneigh = (gself.astype(F32), gneigh.astype(F32))]
    reshape x1 -> x0, local copies, waits for them, and re-layouts: 1.53 us -> none  [on_device(): degree.reshape(nodes, 1)]
where the time goes in v3:
time: 113 us
  Pallas kernels  104 us (92%)
  other arithmetic  3.92 us (3%)
  local copies, waits for them, and re-layouts  3.63 us (3%)
  between operations  1.3 us (1%)
    pallas_call x1, Pallas kernels, on_device(): pl.pallas_call(functools.partial(kernel, n_row, reduce_here), out_shape=(...  104 us
    convert_element_type x2, other arithmetic, on_device(): gself, gneigh = (gself.astype(F32), gneigh.astype(F32))  3.92 us
    unnamed x12, local copies, waits for them, and re-layouts  3.63 us

profile of v3, /device:TPU:1, one launch (start us, length us, event | category | flops | bytes accessed | tf_op | source)
XLA Modules:
  0.0 113.0 jit_solution(5784697189128929527)
XLA Ops:
  1.3 1.4 %copy.14.blist = s32[18,2]{1,0:T(8,128)} copy(s32[18,2]{0,1:T(2,128)} %param.11) | data formatting | bytes 288 | tf_op args[2]
  2.6 104.2 %shard_map.128 = (bf16[512,512]{1,0:T(8,128)(2,1)}, bf16[512,768]{1,0:T(8,128)(2,1)}, bf16[768,512]{1,0:T(8,128)(2,1)}, bf16[768,512]{1,0:T(8,128)(2,1)}, f32[1,512]{1,0:T(1,128)}) custom-call(bf16[512,768]{1,0:T(8,128)(2,1)} %feat.1, s32[4,128]{1,0:T(4,128)} %bitcast.3, s32[18,2]{1,0:T(8,128)} %copy.14.blist, s32[1]{0:T(128)S(6)} %copy.18.bcount, ...), custom_call_target="tpu_custom_call" | custom-call | tf_op jit(solution)/shard_map/pallas_call | solution.py:588
  106.8 0.0 copy-start.1
  106.8 2.6 %convert_element_type.6 = f32[768,512]{1,0:T(8,128)} convert(bf16[768,512]{1,0:T(8,128)(2,1)} %get-tuple-element.12) | non-fusion elementwise | flops 393216 | bytes 2359296 | tf_op jit(solution)/shard_map/convert_element_type | solution.py:615
  109.4 0.0 copy-done.1
  109.4 0.0 copy-start.2
  109.4 0.0 copy-start
  109.4 1.4 %convert_element_type.7 = f32[768,512]{1,0:T(8,128)} convert(bf16[768,512]{1,0:T(8,128)(2,1)S(1)} %copy-done.1) | non-fusion elementwise | flops 393216 | bytes 2359296 | tf_op jit(solution)/shard_map/convert_element_type | solution.py:615
  110.8 0.0 copy-done.2
  110.8 0.0 copy-start.3
  110.8 0.8 copy.19
  111.6 0.0 copy-done
  111.6 0.9 copy.20
  112.4 0.0 copy-done.3
  112.4 0.6 copy.21
Async XLA Ops:
  106.8 2.6 %copy-start.1 = (bf16[768,512]{1,0:T(8,128)(2,1)S(1)}, bf16[768,512]{1,0:T(8,128)(2,1)}, u32[]{:S(2)}) copy-start(bf16[768,512]{1,0:T(8,128)(2,1)} %get-tuple-element.13) | copy-start | bytes 2359300
  109.4 1.4 %copy-start.2 = (bf16[512,512]{1,0:T(8,128)(2,1)S(1)}, bf16[512,512]{1,0:T(8,128)(2,1)}, u32[]{:S(2)}) copy-start(bf16[512,512]{1,0:T(8,128)(2,1)} %get-tuple-element.20) | copy-start | bytes 1572868
  109.4 2.2 %copy-start = (bf16[512,768]{1,0:T(8,128)(2,1)S(1)}, bf16[512,768]{1,0:T(8,128)(2,1)}, u32[]{:S(2)}) copy-start(bf16[512,768]{1,0:T(8,128)(2,1)} %get-tuple-element.21) | copy-start | bytes 2359300
  110.8 1.7 %copy-start.3 = (f32[1,512]{1,0:T(1,128)S(1)}, f32[1,512]{1,0:T(1,128)}, u32[]{:S(2)}) copy-start(f32[1,512]{1,0:T(1,128)} %get-tuple-element.14) | copy-start | bytes 6148

commit v4 on v3

--- a/solution.py
+++ b/solution.py
@@ -10,7 +10,7 @@
 MESH = pl.DeviceIdType.MESH
 F32 = jnp.float32
 BF16 = jnp.bfloat16
-CHUNKS = 4
+CHUNKS = 2
 NEAR = 9
 TANH_SCALE = 0.7978845608028654
 TANH_CUBE = 0.044715
@@ -164,11 +164,7 @@
                 dense_t[b, there, here] = jnp.where(take, flipped, jnp.zeros_like(flipped))
 
     def add_block(b):
-        def body(ch):
-            rows = rows_of(ch)
-            acc[rows, :] += dot(dense[b, rows, :], win[b])
-
-        loop(CHUNKS, body)
+        acc[...] += dot(dense[b], win[b])
 
     def relay(ch):
         fwait(3, ch)
@@ -179,18 +175,14 @@
         fcopy(6, far, 6, ch, partner).start()
 
     def densify_and_relay(ch):
-        densify(2 * ch)
-        densify(2 * ch + 1)
+        for i in range(4):
+            densify(4 * ch + i)
         relay(ch)
 
     loop(CHUNKS, densify_and_relay)
     densify(NEAR - 1)
 
-    def self_part(ch):
-        rows = rows_of(ch)
-        acc[rows, :] = dot(dense[0, rows, :], win[0])
-
-    loop(CHUNKS, self_part)
+    acc[...] = dot(dense[0], win[0])
 
     feat_t[...] = feat[...].T
 
@@ -298,7 +290,6 @@
 
     f_in = feat.shape[1]
     half_f, quarter_f = f_in // 2, f_in // 4
-    f_step = f_in // CHUNKS
 
     width = gloc.shape[2]
 
@@ -444,11 +435,7 @@
     def weight_grad(u, source):
         cols = pl.ds(u % 2 * width, width)
 
-        def body(i):
-            rows = pl.ds(pl.multiple_of(i * f_step, f_step), f_step)
-            gloc[u, rows, :] = dot(feat_t[rows, :], source[:, cols])
-
-        loop(CHUNKS, body)
+        gloc[u] = dot(feat_t[...], source[:, cols])
 
     weight_grad(0, gpre_b)
     if reduce_here:

time: 113 us -> 107 us (0.947)
  Pallas kernels: 104 us -> 96.5 us
  local copies, waits for them, and re-layouts: 3.63 us -> 4.9 us
    pallas_call x1, Pallas kernels: 104 us -> 96.5 us  [on_device(): pl.pallas_call(functools.partial(kernel, n_row, reduce_here), out_shape=(...]
    reshape x0 -> x1, local copies, waits for them, and re-layouts: none -> 1.27 us  [on_device(): degree.reshape(CHUNKS, nodes // CHUNKS)]
where the time goes in v4:
time: 107 us
  Pallas kernels  96.5 us (90%)
  local copies, waits for them, and re-layouts  4.9 us (5%)
  other arithmetic  3.92 us (4%)
  between operations  1.3 us (1%)
    pallas_call x1, Pallas kernels, on_device(): pl.pallas_call(functools.partial(kernel, n_row, reduce_here), out_shape=(...  96.5 us
    convert_element_type x2, other arithmetic, on_device(): gself, gneigh = (gself.astype(F32), gneigh.astype(F32))  3.92 us
    unnamed x12, local copies, waits for them, and re-layouts  3.63 us

profile of v4, /device:TPU:1, one launch (start us, length us, event | category | flops | bytes accessed | tf_op | source)
XLA Modules:
  0.0 106.6 jit_solution(1196275415471403446)
XLA Ops:
  1.3 1.3 %reshape.19.degree = s32[2,256]{1,0:T(2,128)} reshape(s32[512]{0:T(512)} %param.10) | data formatting | bytes 4096 | tf_op jit(solution)/shard_map/reshape | solution.py:592
  2.6 1.4 %copy.14.blist = s32[18,2]{1,0:T(8,128)} copy(s32[18,2]{0,1:T(2,128)} %param.11) | data formatting | bytes 288 | tf_op args[2]
  3.9 96.5 %shard_map.128 = (bf16[512,512]{1,0:T(8,128)(2,1)}, bf16[512,768]{1,0:T(8,128)(2,1)}, bf16[768,512]{1,0:T(8,128)(2,1)}, bf16[768,512]{1,0:T(8,128)(2,1)}, f32[1,512]{1,0:T(1,128)}) custom-call(bf16[512,768]{1,0:T(8,128)(2,1)} %feat.1, s32[2,256]{1,0:T(2,128)} %reshape.19.degree, s32[18,2]{1,0:T(8,128)} %copy.14.blist, s32[1]{0:T(128)S(6)} %copy.18.bcount, ...), custom_call_target="tpu_custom_call" | custom-call | tf_op jit(solution)/shard_map/pallas_call | solution.py:575
  100.4 0.0 copy-start.1
  100.4 2.6 %convert_element_type.6 = f32[768,512]{1,0:T(8,128)} convert(bf16[768,512]{1,0:T(8,128)(2,1)} %get-tuple-element.12) | non-fusion elementwise | flops 393216 | bytes 2359296 | tf_op jit(solution)/shard_map/convert_element_type | solution.py:602
  103.0 0.0 copy-done.1
  103.0 0.0 copy-start.2
  103.0 0.0 copy-start
  103.0 1.4 %convert_element_type.7 = f32[768,512]{1,0:T(8,128)} convert(bf16[768,512]{1,0:T(8,128)(2,1)S(1)} %copy-done.1) | non-fusion elementwise | flops 393216 | bytes 2359296 | tf_op jit(solution)/shard_map/convert_element_type | solution.py:602
  104.4 0.0 copy-done.2
  104.4 0.0 copy-start.3
  104.4 0.8 copy.19
  105.2 0.0 copy-done
  105.2 0.9 copy.20
  106.0 0.0 copy-done.3
  106.0 0.6 copy.21
Async XLA Ops:
  100.4 2.6 %copy-start.1 = (bf16[768,512]{1,0:T(8,128)(2,1)S(1)}, bf16[768,512]{1,0:T(8,128)(2,1)}, u32[]{:S(2)}) copy-start(bf16[768,512]{1,0:T(8,128)(2,1)} %get-tuple-element.13) | copy-start | bytes 2359300
  103.0 1.4 %copy-start.2 = (bf16[512,512]{1,0:T(8,128)(2,1)S(1)}, bf16[512,512]{1,0:T(8,128)(2,1)}, u32[]{:S(2)}) copy-start(bf16[512,512]{1,0:T(8,128)(2,1)} %get-tuple-element.20) | copy-start | bytes 1572868
  103.0 2.2 %copy-start = (bf16[512,768]{1,0:T(8,128)(2,1)S(1)}, bf16[512,768]{1,0:T(8,128)(2,1)}, u32[]{:S(2)}) copy-start(bf16[512,768]{1,0:T(8,128)(2,1)} %get-tuple-element.21) | copy-start | bytes 2359300
  104.4 1.7 %copy-start.3 = (f32[1,512]{1,0:T(1,128)S(1)}, f32[1,512]{1,0:T(1,128)}, u32[]{:S(2)}) copy-start(f32[1,512]{1,0:T(1,128)} %get-tuple-element.14) | copy-start | bytes 6148
